TPU v7x, 512 devices: a whole 4x4x16 slice. The times are simulated.
512 devices in a mesh: grp: 16 (over x, y_hi, core), ep: 32 (over y_lo, z).
Axes of the slice: x: 4, y: 4 (y_hi: 2, y_lo: 2; y = y_hi * 2 + y_lo), z: 16, core: 2. Of those that a mesh axis runs over, the one named last changes fastest.
Arguments:
- tokens: bfloat16 [4096, 3584], P('ep', 'grp'), may hold values from -6 to 6
- routes: int32 [4096, 1], P('ep'), may hold values from 0 to 31; in each aligned block of 128 rows (0 to 127, 128 to 255, ...) at most 8 rows name the same one
- route_weights: float32 [4096, 1], P('ep'), may hold values from 0.2 to 1
- hot_experts: int32 [16], replicated, may hold values from 0 to 15, as said below
- w_gate: bfloat16 [16, 3584, 2048], P(None, 'ep', 'grp'), may hold values from -0.09375 to 0.09375
- w_up: bfloat16 [16, 3584, 2048], P(None, 'ep', 'grp'), may hold values from -0.09375 to 0.09375
- w_down: bfloat16 [16, 2048, 3584], P(None, 'grp', 'ep'), may hold values from -0.125 to 0.125
- cotangent: bfloat16 [4096, 3584], P('ep', 'grp'), may hold values from -3 to 3
Outputs:
- layer_output: bfloat16 [4096, 3584], P('ep', 'grp')
- grad_tokens: bfloat16 [4096, 3584], P('ep', 'grp')
- grad_gate: bfloat16 [16, 3584, 2048], P(None, 'ep', 'grp')
- grad_up: bfloat16 [16, 3584, 2048], P(None, 'ep', 'grp')
- grad_down: bfloat16 [16, 2048, 3584], P(None, 'grp', 'ep')
Inputs may be any that keep to these rules, and one draw needn't show every extreme that they name: `routes`: each row names one slot. Among the rows of one device (aligned blocks of 128 rows) no slot is named by more than 8 rows. `hot_experts`: entry j is the expert held by slot 16 + j; an expert may appear several times.
All inputs are finite; a program needn't handle non-finite values.
Results may differ from a plain program's by a relative error of at most 0.02.
Values may be sent and summed in bfloat16 or wider, within the bound.
A program may use at most 64 MiB of HBM per device.

v0:
```python
import jax
import jax.numpy as jnp
from jax import lax
from jax.sharding import PartitionSpec as P


def shards(tokens, routes, route_weights, hot_experts, w_gate, w_up, w_down, cotangent):
    ep_size = lax.axis_size("ep")
    tok_count = tokens.shape[0]
    top_count = routes.shape[1]
    flat_count = tok_count * top_count
    capacity = 2 * flat_count // ep_size
    pad_rows = ep_size * capacity
    expert_count = w_gate.shape[0]
    hidden = w_gate.shape[2]
    stored = w_gate.shape[1]
    width = stored * ep_size
    slot_host = jnp.concatenate([jnp.arange(expert_count, dtype=jnp.int32), hot_experts])
    flat_slot = routes.reshape(-1)
    onehot = (flat_slot[:, None] == jnp.arange(ep_size, dtype=jnp.int32)[None, :]).astype(jnp.int32)
    before = jnp.cumsum(onehot, axis=0) - onehot
    position = jnp.sum(before * onehot, axis=1)
    dest = flat_slot * capacity + position
    source = (
        jnp.full((pad_rows,), flat_count, jnp.int32)
        .at[dest]
        .set(jnp.arange(flat_count, dtype=jnp.int32))
    )
    token_of = source // top_count
    flat_weights = route_weights.reshape(-1)
    weight_of = jnp.take(jnp.concatenate([flat_weights, jnp.zeros((1,), jnp.float32)]), source)
    sel_gate = jnp.take(w_gate, slot_host, axis=0)
    sel_up = jnp.take(w_up, slot_host, axis=0)
    sel_down = jnp.swapaxes(jnp.take(w_down, slot_host, axis=0), 1, 2)
    packed = jnp.concatenate([sel_gate, sel_up, sel_down], axis=2)
    received = lax.all_to_all(packed, "ep", split_axis=0, concat_axis=0, tiled=True)
    slot_weights = received.reshape(width, 3 * hidden)
    gate_up_w = slot_weights[:, : 2 * hidden]
    down_t = slot_weights[:, 2 * hidden :]

    def pick_rows(source_table, route_scale):
        extended = jnp.concatenate(
            [source_table, jnp.zeros((1, source_table.shape[1]), source_table.dtype)], axis=0
        )
        picked = jnp.take(extended, token_of, axis=0)
        if route_scale is not None:
            picked = (picked.astype(jnp.float32) * route_scale[:, None]).astype(jnp.bfloat16)
        return picked

    def deliver(source_table, route_scale):
        send_rows = pick_rows(source_table, route_scale)
        moved = lax.all_to_all(
            send_rows.reshape(ep_size, capacity, -1), "ep", split_axis=0, concat_axis=0, tiled=True
        )
        return lax.all_gather(moved.reshape(pad_rows, -1), "grp", axis=1, tiled=True)

    def combine(part_rows, weighted):
        block_sum = lax.psum_scatter(
            part_rows.astype(jnp.float32).astype(jnp.bfloat16),
            "grp",
            scatter_dimension=1,
            tiled=True,
        ).astype(jnp.float32)
        returned = lax.all_to_all(
            block_sum.reshape(ep_size, capacity, -1).astype(jnp.bfloat16),
            "ep",
            split_axis=0,
            concat_axis=0,
            tiled=True,
        ).astype(jnp.float32)
        route_rows = jnp.take(returned.reshape(pad_rows, -1), dest, axis=0)
        if weighted:
            route_rows = route_rows * flat_weights[:, None]
        return jnp.sum(route_rows.reshape(tok_count, top_count, -1), axis=1)

    contract_last = (((1,), (1,)), ((), ()))
    contract_first = (((0,), (0,)), ((), ()))
    x_rows = deliver(tokens, None)
    gate_up = jnp.dot(x_rows, gate_up_w, preferred_element_type=jnp.float32)
    gate_pre = gate_up[:, :hidden]
    up_pre = gate_up[:, hidden:]
    sigmoid_gate = jax.nn.sigmoid(gate_pre)
    act = (gate_pre * sigmoid_gate * up_pre).astype(jnp.bfloat16)
    out_parts = lax.dot_general(
        act, down_t, contract_last, preferred_element_type=jnp.float32
    ).astype(jnp.bfloat16)
    layer_output = combine(out_parts, True).astype(jnp.bfloat16)
    dz_rows = deliver(cotangent, weight_of)
    act_grad = jnp.dot(dz_rows, down_t, preferred_element_type=jnp.float32)
    gate_grad = act_grad * up_pre * sigmoid_gate * (1.0 + gate_pre * (1.0 - sigmoid_gate))
    up_grad = act_grad * gate_pre * sigmoid_gate
    pre_grad = jnp.concatenate([gate_grad, up_grad], axis=1).astype(jnp.bfloat16)
    tok_parts = lax.dot_general(
        pre_grad, gate_up_w, contract_last, preferred_element_type=jnp.float32
    ).astype(jnp.bfloat16)
    grad_tokens = combine(tok_parts, False).astype(jnp.bfloat16)
    grad_gate_up = lax.dot_general(
        x_rows, pre_grad, contract_first, preferred_element_type=jnp.float32
    )
    grad_down_t = lax.dot_general(dz_rows, act, contract_first, preferred_element_type=jnp.float32)
    slot_grad = jnp.concatenate([grad_gate_up, grad_down_t], axis=1).astype(jnp.bfloat16)
    owner_pieces = lax.all_to_all(
        slot_grad.reshape(ep_size, stored, 3 * hidden),
        "ep",
        split_axis=0,
        concat_axis=0,
        tiled=True,
    )
    host_onehot = (slot_host[None, :] == jnp.arange(expert_count, dtype=jnp.int32)[:, None]).astype(
        jnp.bfloat16
    )
    totals = jnp.einsum(
        "es,sdh->edh", host_onehot, owner_pieces, preferred_element_type=jnp.float32
    )
    grad_gate = totals[:, :, :hidden].astype(jnp.bfloat16)
    grad_up = totals[:, :, hidden : 2 * hidden].astype(jnp.bfloat16)
    grad_down = jnp.swapaxes(totals[:, :, 2 * hidden :], 1, 2).astype(jnp.bfloat16)
    return (layer_output, grad_tokens, grad_gate, grad_up, grad_down)


def solution(mesh):
    placed = (
        P("ep", "grp"),
        P("ep", None),
        P("ep", None),
        P(),
        P(None, "ep", "grp"),
        P(None, "ep", "grp"),
        P(None, "grp", "ep"),
        P("ep", "grp"),
    )
    return jax.shard_map(
        shards,
        mesh=mesh,
        in_specs=placed,
        out_specs=(
            P("ep", "grp"),
            P("ep", "grp"),
            P(None, "ep", "grp"),
            P(None, "ep", "grp"),
            P(None, "grp", "ep"),
        ),
        check_vma=False,
    )
```

profile of v0, /device:TPU:32, one launch (start us, length us, event | category | flops | bytes accessed | tf_op | source)
XLA Modules:
  0.0 573.1 jit_solution(13646672877807859614)
XLA Ops:
  7.2 0.8 fusion.13
  8.0 0.2 reduce_window_sum.11
  8.2 0.8 select_reduce_fusion
  9.0 0.7 fusion.17
  9.7 1.0 scatter_custom_fusion
  10.7 0.7 pad_maximum_fusion.5
  11.4 1.9 gather_fusion.1
  13.3 0.9 copy.47
  14.3 1.2 gather_fusion.2
  15.4 0.8 select_bitcast_fusion.1
  16.2 16.4 %all-to-all-start = ((bf16[32,8,224]{2,1,0:T(8,128)(2,1)}), bf16[32,8,224]{2,1,0:T(8,128)(2,1)S(1)}, u32[]{:S(2)}, u32[]{:S(2)}) async-start(bf16[32,8,224]{2,1,0:T(8,128)(2,1)} %select_bitcast_fusion.1), calls=%async_computation | async-start | bytes 262144 | tf_op jit(solution)/shard_map/all_to_all | solution.py:52
  32.6 0.1 compare_select_fusion.2
  32.7 0.7 gather_fusion.4
  33.4 0.7 gather_fusion.3
  34.2 0.1 fusion.18
  34.3 0.1 copy.50
  34.4 1.2 gather_fusion.6
  35.5 1.7 gather_fusion
  37.3 0.8 fusion.11
  38.1 1.5 broadcast_select_fusion.1
  39.6 8.8 %all-to-all-done = bf16[32,8,224]{2,1,0:T(8,128)(2,1)S(1)} async-done(((bf16[32,8,224]{2,1,0:T(8,128)(2,1)}), bf16[32,8,224]{2,1,0:T(8,128)(2,1)S(1)}, u32[]{:S(2)}, u32[]{:S(2)}) %all-to-all-start) | async-done | bytes 114720 | tf_op jit(solution)/shard_map/all_to_all | solution.py:52
  48.4 4.7 all-to-all-start.3
  53.2 0.2 select_bitcast_fusion
  53.3 3.4 pad_maximum_fusion
  56.7 11.4 %all-to-all-done.3 = bf16[32,8,224]{2,1,0:T(8,128)(2,1)S(1)} async-done(((bf16[32,8,224]{2,1,0:T(8,128)(2,1)}), bf16[32,8,224]{2,1,0:T(8,128)(2,1)S(1)}, u32[]{:S(2)}, u32[]{:S(2)}) %all-to-all-start.3) | async-done | bytes 114720 | tf_op jit(solution)/shard_map/all_to_all | solution.py:52
  68.1 4.9 all-to-all-start.1
  73.1 0.0 all-gather.3.cloned.1.call-start
  73.1 0.8 copy.48
  73.9 0.0 all-gather.5.cloned.1.call-start
  73.9 0.8 copy.51
  74.7 0.0 reduce-scatter.5.cloned.1.call-start
  74.8 69.1 %all-gather.3.cloned.1.call-done = bf16[256,3584]{0,1:T(8,128)(2,1)} async-done(((bf16[256,224]{0,1:T(8,128)(2,1)}), bf16[256,3584]{0,1:T(8,128)(2,1)}) %all-gather.3.cloned.1.call-update) | async-done | bytes 1835024 | tf_op jit(solution)/shard_map/all_gather | solution.py:55
  143.9 53.7 %all-to-all-done.1 = bf16[32,112,384]{2,1,0:T(8,128)(2,1)S(1)} async-done(((bf16[32,112,384]{2,1,0:T(8,128)(2,1)}), bf16[32,112,384]{2,1,0:T(8,128)(2,1)S(1)}, u32[]{:S(2)}, u32[]{:S(2)}) %all-to-all-start.1) | async-done | bytes 2752544 | tf_op jit(solution)/shard_map/all_to_all | solution.py:36
  197.6 3.0 fusion.6
  200.6 10.0 %all-gather.5.cloned.1.call-done = bf16[256,3584]{0,1:T(8,128)(2,1)} async-done(((bf16[256,224]{0,1:T(8,128)(2,1)}), bf16[256,3584]{0,1:T(8,128)(2,1)}) %all-gather.5.cloned.1.call-update) | async-done | bytes 1835024 | tf_op jit(solution)/shard_map/all_gather | solution.py:55
  210.6 2.1 multiply_convert_fusion.2
  212.7 1.9 convolution_convert_fusion.1
  214.7 0.0 reduce-scatter.3.cloned.1.call-start
  214.7 1.9 convolution_convert_fusion
  216.6 89.9 %reduce-scatter.5.cloned.1.call-done = bf16[256,224]{0,1:T(8,128)(2,1)} async-done(((bf16[256,3584]{0,1:T(8,128)(2,1)}), bf16[256,224]{0,1:T(8,128)(2,1)}) %reduce-scatter.5.cloned.1.call-update) | async-done | bytes 114704 | tf_op jit(solution)/shard_map/reduce_scatter | solution.py:58
  306.5 1.7 copy.52
  308.2 13.0 %all-to-all-start.4 = ((bf16[32,8,224]{2,1,0:T(8,128)(2,1)}), bf16[32,8,224]{2,1,0:T(8,128)(2,1)S(1)}, u32[]{:S(2)}, u32[]{:S(2)}) async-start(bf16[32,8,224]{2,1,0:T(8,128)(2,1)} %bitcast.14), calls=%async_computation.6 | async-start | bytes 262144 | tf_op jit(solution)/shard_map/all_to_all | solution.py:64
  321.2 2.2 convolution_convert_fusion.2
  323.3 80.7 %reduce-scatter.3.cloned.1.call-done = bf16[256,224]{0,1:T(8,128)(2,1)} async-done(((bf16[256,3584]{0,1:T(8,128)(2,1)}), bf16[256,224]{0,1:T(8,128)(2,1)}) %reduce-scatter.3.cloned.1.call-update) | async-done | bytes 114704 | tf_op jit(solution)/shard_map/reduce_scatter | solution.py:58
  404.1 1.7 copy.49
  405.7 13.0 %all-to-all-start.2 = ((bf16[32,8,224]{2,1,0:T(8,128)(2,1)}), bf16[32,8,224]{2,1,0:T(8,128)(2,1)S(1)}, u32[]{:S(2)}, u32[]{:S(2)}) async-start(bf16[32,8,224]{2,1,0:T(8,128)(2,1)} %bitcast.9), calls=%async_computation.3 | async-start | bytes 262144 | tf_op jit(solution)/shard_map/all_to_all | solution.py:64
  418.8 2.1 convolution_convert_fusion.3
  420.9 1.8 pad_maximum_fusion.1
  422.7 10.6 %all-to-all-done.2 = bf16[32,8,224]{2,1,0:T(8,128)(2,1)S(1)} async-done(((bf16[32,8,224]{2,1,0:T(8,128)(2,1)}), bf16[32,8,224]{2,1,0:T(8,128)(2,1)S(1)}, u32[]{:S(2)}, u32[]{:S(2)}) %all-to-all-start.2) | async-done | bytes 114720 | tf_op jit(solution)/shard_map/all_to_all | solution.py:64
  433.3 0.7 copy-done.2
  434.0 4.9 all-to-all-start.5
  439.0 0.8 gather_fusion.7
  439.8 0.1 select_convert_fusion
  439.9 0.7 copy.55
  440.6 0.9 bitcast_convert_fusion.1
  441.6 1.4 gather_fusion.5
  443.0 1.0 fusion.12
  444.0 0.7 copy.54
  444.7 118.4 %all-to-all-done.5 = bf16[32,112,384]{2,1,0:T(8,128)(2,1)S(1)} async-done(((bf16[32,112,384]{2,1,0:T(8,128)(2,1)}), bf16[32,112,384]{2,1,0:T(8,128)(2,1)S(1)}, u32[]{:S(2)}, u32[]{:S(2)}) %all-to-all-start.5) | async-done | bytes 2752544 | tf_op jit(solution)/shard_map/all_to_all | solution.py:102
  563.1 0.6 fusion.2
  563.7 0.2 slice_bitcast_fusion
  563.9 0.9 copy.56
  564.8 0.9 copy.57
  565.7 0.9 copy.58
  (31 shorter events, 0.2 us)
Async XLA Ops:
  7.2 25.5 %copy-start = (bf16[16,112,128]{2,1,0:T(8,128)(2,1)S(1)}, bf16[16,112,128]{2,1,0:T(8,128)(2,1)}, u32[]{:S(2)}) copy-start(bf16[16,112,128]{2,1,0:T(8,128)(2,1)} %param.19) | copy-start | bytes 1376260
  7.2 25.4 %copy-start.6 = (s32[16]{0:T(128)S(1)}, s32[16]{0:T(128)}, u32[]{:S(2)}) copy-start(s32[16]{0:T(128)} %param.17) | copy-start | bytes 196
  7.2 26.2 %copy-start.1 = (bf16[16,112,128]{2,1,0:T(8,128)(2,1)S(1)}, bf16[16,112,128]{2,1,0:T(8,128)(2,1)}, u32[]{:S(2)}) copy-start(bf16[16,112,128]{2,1,0:T(8,128)(2,1)} %param.18) | copy-start | bytes 1376260
  14.3 20.0 %copy-start.3 = (bf16[128,224]{0,1:T(8,128)(2,1)S(1)}, bf16[128,224]{0,1:T(8,128)(2,1)}, u32[]{:S(2)}) copy-start(bf16[128,224]{0,1:T(8,128)(2,1)} %param.21) | copy-start | bytes 172036
  16.2 32.2 %all-to-all-start = ((bf16[32,8,224]{2,1,0:T(8,128)(2,1)}), bf16[32,8,224]{2,1,0:T(8,128)(2,1)S(1)}, u32[]{:S(2)}, u32[]{:S(2)}) async-start(bf16[32,8,224]{2,1,0:T(8,128)(2,1)} %select_bitcast_fusion.1), calls=%async_computation | async-start | bytes 262144 | tf_op jit(solution)/shard_map/all_to_all | solution.py:52
  48.4 19.7 %all-to-all-start.3 = ((bf16[32,8,224]{2,1,0:T(8,128)(2,1)}), bf16[32,8,224]{2,1,0:T(8,128)(2,1)S(1)}, u32[]{:S(2)}, u32[]{:S(2)}) async-start(bf16[32,8,224]{2,1,0:T(8,128)(2,1)} %fusion.11), calls=%async_computation.4 | async-start | bytes 262144 | tf_op jit(solution)/shard_map/all_to_all | solution.py:52
  68.1 129.4 %all-to-all-start.1 = ((bf16[32,112,384]{2,1,0:T(8,128)(2,1)}), bf16[32,112,384]{2,1,0:T(8,128)(2,1)S(1)}, u32[]{:S(2)}, u32[]{:S(2)}) async-start(bf16[32,112,384]{2,1,0:T(8,128)(2,1)} %pad_maximum_fusion), calls=%async_computation.1 | async-start | bytes 5505024 | tf_op jit(solution)/shard_map/all_to_all | solution.py:36
  73.1 70.8 %all-gather.3.cloned.1.call-start = ((), (), s32[]{:S(2)}) async-start(), calls=%async_computation.8 | async-start | bytes 1949696 | tf_op jit(solution)/shard_map/all_gather | solution.py:55
  73.9 136.8 %all-gather.5.cloned.1.call-start = ((), (), s32[]{:S(2)}) async-start(), calls=%async_computation.10 | async-start | bytes 1949696 | tf_op jit(solution)/shard_map/all_gather | solution.py:55
  74.7 231.8 %reduce-scatter.5.cloned.1.call-start = ((), (), s32[]{:S(2)}) async-start(), calls=%async_computation.11 | async-start | bytes 1949696 | tf_op jit(solution)/shard_map/reduce_scatter | solution.py:58
  214.7 189.4 %reduce-scatter.3.cloned.1.call-start = ((), (), s32[]{:S(2)}) async-start(), calls=%async_computation.9 | async-start | bytes 1949696 | tf_op jit(solution)/shard_map/reduce_scatter | solution.py:58
  308.2 97.5 %all-to-all-start.4 = ((bf16[32,8,224]{2,1,0:T(8,128)(2,1)}), bf16[32,8,224]{2,1,0:T(8,128)(2,1)S(1)}, u32[]{:S(2)}, u32[]{:S(2)}) async-start(bf16[32,8,224]{2,1,0:T(8,128)(2,1)} %bitcast.14), calls=%async_computation.6 | async-start | bytes 262144 | tf_op jit(solution)/shard_map/all_to_all | solution.py:64
  405.7 27.6 %all-to-all-start.2 = ((bf16[32,8,224]{2,1,0:T(8,128)(2,1)}), bf16[32,8,224]{2,1,0:T(8,128)(2,1)S(1)}, u32[]{:S(2)}, u32[]{:S(2)}) async-start(bf16[32,8,224]{2,1,0:T(8,128)(2,1)} %bitcast.9), calls=%async_computation.3 | async-start | bytes 262144 | tf_op jit(solution)/shard_map/all_to_all | solution.py:64
  422.7 16.2 %copy-start.4 = (s32[128,1]{0,1:T(1,128)S(1)}, s32[128,1]{0,1:T(1,128)}, u32[]{:S(2)}) copy-start(s32[128,1]{0,1:T(1,128)} %param.15) | copy-start | bytes 1540
  422.7 20.3 %copy-start.5 = (f32[128,1]{0,1:T(1,128)S(1)}, f32[128,1]{0,1:T(1,128)}, u32[]{:S(2)}) copy-start(f32[128,1]{0,1:T(1,128)} %param.16) | copy-start | bytes 1540
  433.3 0.7 copy-start.2
  434.0 129.1 %all-to-all-start.5 = ((bf16[32,112,384]{2,1,0:T(8,128)(2,1)}), bf16[32,112,384]{2,1,0:T(8,128)(2,1)S(1)}, u32[]{:S(2)}, u32[]{:S(2)}) async-start(bf16[32,112,384]{2,1,0:T(8,128)(2,1)} %pad_maximum_fusion.1), calls=%async_computation.7 | async-start | bytes 5505024 | tf_op jit(solution)/shard_map/all_to_all | solution.py:102
Sparse Core Ops, SparseCore 0:
  77.7 66.0 all-gather.2
  147.7 62.8 all-gather.4
  215.4 91.0 reduce-scatter.4
  311.9 92.1 reduce-scatter.2
where the time goes:
time: 574 us; the launch traced here: 573 us
  waiting for transfers between devices  453 us (79%)
  starting transfers between devices  57.1 us (10%)
  local copies, waits for them, and re-layouts  21.6 us (4%)
  between operations  14.1 us (2%)
  other arithmetic  13.8 us (2%)
  matrix products  13.8 us (2%)
    reduce_scatter x2, waiting for transfers between devices, combine(): lax.psum_scatter(part_rows.astype(jnp.float32).astype(jnp.bfloat16), 'grp...  171 us
    all_to_all x1, waiting for transfers between devices, shards(): lax.all_to_all(slot_grad.reshape(ep_size, stored, 3 * hidden), 'ep', spli...  118 us
    all_gather x2, waiting for transfers between devices, deliver(): lax.all_gather(moved.reshape(pad_rows, -1), 'grp', axis=1, tiled=True)  79.1 us
    all_to_all x1, waiting for transfers between devices, shards(): lax.all_to_all(packed, 'ep', split_axis=0, concat_axis=0, tiled=True)  53.7 us
    all_to_all x2, starting transfers between devices, combine(): lax.all_to_all(block_sum.reshape(ep_size, capacity, -1).astype(jnp.bfloat...  26 us
    all_to_all x2, starting transfers between devices, deliver(): lax.all_to_all(send_rows.reshape(ep_size, capacity, -1), 'ep', split_axis...  21.1 us
    all_to_all x2, waiting for transfers between devices, deliver(): lax.all_to_all(send_rows.reshape(ep_size, capacity, -1), 'ep', split_axis...  20.2 us
  transfers between devices with their start and end apart: 10, of which 9 were waited for; matrix products, arithmetic and copies ran while one was open for 6% of the time, Pallas kernels for 0%

commit v1 on v0

--- a/solution.py
+++ b/solution.py
@@ -52,7 +52,12 @@
         moved = lax.all_to_all(
             send_rows.reshape(ep_size, capacity, -1), "ep", split_axis=0, concat_axis=0, tiled=True
         )
-        return lax.all_gather(moved.reshape(pad_rows, -1), "grp", axis=1, tiled=True)
+        return jnp.concatenate(
+            lax.all_to_all(
+                jnp.stack([moved.reshape(pad_rows, -1)] * lax.axis_size("grp")), "grp", 0, 0
+            ),
+            axis=1,
+        )
 
     def combine(part_rows, weighted):
         block_sum = lax.psum_scatter(

time: 574 us -> 625 us (1.089)
  waiting for transfers between devices: 453 us -> 486 us
  starting transfers between devices: 57.1 us -> 69.9 us
  local copies, waits for them, and re-layouts: 21.6 us -> 28.7 us
    all_gather x2 -> x0, waiting for transfers between devices: 79.1 us -> none  [deliver(): lax.all_gather(moved.reshape(pad_rows, -1), 'grp', axis=1, tiled=True)]
    all_to_all x1, waiting for transfers between devices: 53.7 us -> 127 us  [shards(): lax.all_to_all(packed, 'ep', split_axis=0, concat_axis=0, tiled=True)]
    all_to_all x0 -> x2, waiting for transfers between devices: none -> 40.9 us  [deliver(): lax.all_to_all(jnp.stack([moved.reshape(pad_rows, -1)] * lax.axis_size('g...]
    all_to_all x0 -> x2, starting transfers between devices: none -> 12.8 us  [deliver(): lax.all_to_all(jnp.stack([moved.reshape(pad_rows, -1)] * lax.axis_size('g...]
    reduce_scatter x2, waiting for transfers between devices: 171 us -> 162 us  [combine(): lax.psum_scatter(part_rows.astype(jnp.float32).astype(jnp.bfloat16), 'grp...]
    all_to_all x2, waiting for transfers between devices: 20.2 us -> 28.3 us  [deliver(): lax.all_to_all(send_rows.reshape(ep_size, capacity, -1), 'ep', split_axis...]
  transfers between devices with their start and end apart: 10 -> 10, of which waited for: 9 -> 9; matrix products, arithmetic and copies ran while one was open for 6% -> 5% of each run, Pallas kernels for 0% -> 0%
where the time goes in v1:
time: 625 us; the launch traced here: 624 us
  waiting for transfers between devices  486 us (78%)
  starting transfers between devices  69.9 us (11%)
  local copies, waits for them, and re-layouts  28.7 us (5%)
  between operations  14.4 us (2%)
  matrix products  14 us (2%)
  other arithmetic  11 us (2%)
    reduce_scatter x2, waiting for transfers between devices, combine(): lax.psum_scatter(part_rows.astype(jnp.float32).astype(jnp.bfloat16), 'grp...  162 us
    all_to_all x1, waiting for transfers between devices, shards(): lax.all_to_all(packed, 'ep', split_axis=0, concat_axis=0, tiled=True)  127 us
    all_to_all x1, waiting for transfers between devices, shards(): lax.all_to_all(slot_grad.reshape(ep_size, stored, 3 * hidden), 'ep', spli...  118 us
    all_to_all x2, waiting for transfers between devices, deliver(): lax.all_to_all(jnp.stack([moved.reshape(pad_rows, -1)] * lax.axis_size('g...  40.9 us
    all_to_all x2, waiting for transfers between devices, deliver(): lax.all_to_all(send_rows.reshape(ep_size, capacity, -1), 'ep', split_axis...  28.3 us
    all_to_all x2, starting transfers between devices, combine(): lax.all_to_all(block_sum.reshape(ep_size, capacity, -1).astype(jnp.bfloat...  26 us
    all_to_all x2, starting transfers between devices, deliver(): lax.all_to_all(send_rows.reshape(ep_size, capacity, -1), 'ep', split_axis...  21.1 us
    all_to_all x2, starting transfers between devices, deliver(): lax.all_to_all(jnp.stack([moved.reshape(pad_rows, -1)] * lax.axis_size('g...  12.8 us
  transfers between devices with their start and end apart: 10, of which 9 were waited for; matrix products, arithmetic and copies ran while one was open for 5% of the time, Pallas kernels for 0%

profile of v1, /device:TPU:32, one launch (start us, length us, event | category | flops | bytes accessed | tf_op | source)
XLA Modules:
  0.0 624.2 jit_solution(3833078991277965114)
XLA Ops:
  7.2 0.8 fusion.25
  8.0 0.2 reduce_window_sum.11
  8.2 0.8 select_reduce_fusion
  9.0 0.7 fusion.29
  9.7 1.0 scatter_custom_fusion
  10.7 0.7 pad_maximum_fusion.5
  11.4 1.9 gather_fusion.1
  13.3 0.9 copy.33
  14.3 1.2 gather_fusion.2
  15.4 0.8 select_bitcast_fusion.1
  16.2 16.4 %all-to-all-start = ((bf16[32,8,224]{2,1,0:T(8,128)(2,1)}), bf16[32,8,224]{2,1,0:T(8,128)(2,1)S(1)}, u32[]{:S(2)}, u32[]{:S(2)}) async-start(bf16[32,8,224]{2,1,0:T(8,128)(2,1)} %select_bitcast_fusion.1), calls=%async_computation | async-start | bytes 262144 | tf_op jit(solution)/shard_map/all_to_all | solution.py:52
  32.6 0.1 copy.36
  32.7 1.2 gather_fusion.6
  33.8 0.8 fusion.21
  34.6 13.8 %all-to-all-done = bf16[32,8,224]{2,1,0:T(8,128)(2,1)S(1)} async-done(((bf16[32,8,224]{2,1,0:T(8,128)(2,1)}), bf16[32,8,224]{2,1,0:T(8,128)(2,1)S(1)}, u32[]{:S(2)}, u32[]{:S(2)}) %all-to-all-start) | async-done | bytes 114720 | tf_op jit(solution)/shard_map/all_to_all | solution.py:52
  48.4 4.7 all-to-all-start.4
  53.2 0.1 copy.34
  53.3 14.5 %all-to-all-done.4 = bf16[32,8,224]{2,1,0:T(8,128)(2,1)S(1)} async-done(((bf16[32,8,224]{2,1,0:T(8,128)(2,1)}), bf16[32,8,224]{2,1,0:T(8,128)(2,1)S(1)}, u32[]{:S(2)}, u32[]{:S(2)}) %all-to-all-start.4) | async-done | bytes 114720 | tf_op jit(solution)/shard_map/all_to_all | solution.py:52
  67.8 1.5 stack.6
  69.3 6.9 %all-to-all-start.1 = ((bf16[16,256,224]{1,2,0:T(8,128)(2,1)}), bf16[16,256,224]{1,2,0:T(8,128)(2,1)S(1)}, u32[]{:S(2)}, u32[]{:S(2)}) async-start(bf16[16,256,224]{1,2,0:T(8,128)(2,1)} %stack.6), calls=%async_computation.1 | async-start | bytes 3670016 | tf_op jit(solution)/shard_map/all_to_all | solution.py:56
  76.2 1.6 gather_fusion.4
  77.8 1.6 gather_fusion.3
  79.5 1.7 gather_fusion
  81.3 0.2 select_bitcast_fusion
  81.5 1.7 broadcast_select_fusion.1
  83.2 1.9 pad_maximum_fusion
  85.1 17.5 %all-to-all-done.1 = bf16[16,256,224]{1,2,0:T(8,128)(2,1)S(1)} async-done(((bf16[16,256,224]{1,2,0:T(8,128)(2,1)}), bf16[16,256,224]{1,2,0:T(8,128)(2,1)S(1)}, u32[]{:S(2)}, u32[]{:S(2)}) %all-to-all-start.1) | async-done | bytes 1835040 | tf_op jit(solution)/shard_map/all_to_all | solution.py:56
  102.5 1.2 copy-done.1
  103.8 5.0 all-to-all-start.2
  108.7 0.1 copy.37
  108.8 127.3 %all-to-all-done.2 = bf16[32,112,384]{2,1,0:T(8,128)(2,1)S(1)} async-done(((bf16[32,112,384]{2,1,0:T(8,128)(2,1)}), bf16[32,112,384]{2,1,0:T(8,128)(2,1)S(1)}, u32[]{:S(2)}, u32[]{:S(2)}) %all-to-all-start.2) | async-done | bytes 2752544 | tf_op jit(solution)/shard_map/all_to_all | solution.py:36
  236.2 1.4 stack.7
  237.6 5.9 all-to-all-start.5
  243.6 3.0 fusion.13
  246.6 23.4 %all-to-all-done.5 = bf16[16,256,224]{1,2,0:T(8,128)(2,1)} async-done(((bf16[16,256,224]{1,2,0:T(8,128)(2,1)}), bf16[16,256,224]{1,2,0:T(8,128)(2,1)}, u32[]{:S(2)}, u32[]{:S(2)}) %all-to-all-start.5) | async-done | bytes 1835040 | tf_op jit(solution)/shard_map/all_to_all | solution.py:56
  270.0 2.1 multiply_convert_fusion.2
  272.1 1.9 convolution_convert_fusion.1
  274.1 1.9 convolution_convert_fusion
  276.0 81.2 %reduce-scatter.5.cloned.1.call-done = bf16[256,224]{0,1:T(8,128)(2,1)} async-done(((bf16[256,3584]{0,1:T(8,128)(2,1)}), bf16[256,224]{0,1:T(8,128)(2,1)}) %reduce-scatter.5.cloned.1.call-update) | async-done | bytes 114704 | tf_op jit(solution)/shard_map/reduce_scatter | solution.py:63
  357.2 1.7 copy.38
  358.8 13.0 %all-to-all-start.6 = ((bf16[32,8,224]{2,1,0:T(8,128)(2,1)}), bf16[32,8,224]{2,1,0:T(8,128)(2,1)S(1)}, u32[]{:S(2)}, u32[]{:S(2)}) async-start(bf16[32,8,224]{2,1,0:T(8,128)(2,1)} %bitcast.18), calls=%async_computation.8 | async-start | bytes 262144 | tf_op jit(solution)/shard_map/all_to_all | solution.py:69
  371.8 2.3 fusion.6
  374.1 80.8 %reduce-scatter.3.cloned.1.call-done = bf16[256,224]{0,1:T(8,128)(2,1)} async-done(((bf16[256,3584]{0,1:T(8,128)(2,1)}), bf16[256,224]{0,1:T(8,128)(2,1)}) %reduce-scatter.3.cloned.1.call-update) | async-done | bytes 114704 | tf_op jit(solution)/shard_map/reduce_scatter | solution.py:63
  454.9 1.7 copy.35
  456.6 13.0 %all-to-all-start.3 = ((bf16[32,8,224]{2,1,0:T(8,128)(2,1)}), bf16[32,8,224]{2,1,0:T(8,128)(2,1)S(1)}, u32[]{:S(2)}, u32[]{:S(2)}) async-start(bf16[32,8,224]{2,1,0:T(8,128)(2,1)} %bitcast.11), calls=%async_computation.4 | async-start | bytes 262144 | tf_op jit(solution)/shard_map/all_to_all | solution.py:69
  469.6 2.2 fusion.15
  471.8 0.3 pad_maximum_fusion.1
  472.1 2.5 copy.43
  474.7 9.5 %all-to-all-done.3 = bf16[32,8,224]{2,1,0:T(8,128)(2,1)S(1)} async-done(((bf16[32,8,224]{2,1,0:T(8,128)(2,1)}), bf16[32,8,224]{2,1,0:T(8,128)(2,1)S(1)}, u32[]{:S(2)}, u32[]{:S(2)}) %all-to-all-start.3) | async-done | bytes 114720 | tf_op jit(solution)/shard_map/all_to_all | solution.py:69
  484.1 0.7 copy-done.3
  484.8 4.9 all-to-all-start.7
  489.8 0.8 gather_fusion.7
  490.6 0.1 select_convert_fusion
  490.7 0.7 copy.46
  491.4 0.9 bitcast_convert_fusion.1
  492.4 1.4 gather_fusion.5
  493.8 1.0 fusion.23
  494.8 0.7 copy.45
  495.5 118.4 %all-to-all-done.7 = bf16[32,112,384]{2,1,0:T(8,128)(2,1)S(1)} async-done(((bf16[32,112,384]{2,1,0:T(8,128)(2,1)}), bf16[32,112,384]{2,1,0:T(8,128)(2,1)S(1)}, u32[]{:S(2)}, u32[]{:S(2)}) %all-to-all-start.7) | async-done | bytes 2752544 | tf_op jit(solution)/shard_map/all_to_all | solution.py:107
  613.9 0.6 fusion.9
  614.5 0.2 slice_bitcast_fusion
  614.7 0.9 copy.47
  615.6 0.9 copy.48
  616.5 0.9 copy.49
  (34 shorter events, 0.4 us)
Async XLA Ops:
  7.2 69.1 %copy-start = (bf16[16,112,128]{2,1,0:T(8,128)(2,1)S(1)}, bf16[16,112,128]{2,1,0:T(8,128)(2,1)}, u32[]{:S(2)}) copy-start(bf16[16,112,128]{2,1,0:T(8,128)(2,1)} %param.19) | copy-start | bytes 1376260
  7.2 25.4 %copy-start.4 = (bf16[128,224]{0,1:T(8,128)(2,1)S(1)}, bf16[128,224]{0,1:T(8,128)(2,1)}, u32[]{:S(2)}) copy-start(bf16[128,224]{0,1:T(8,128)(2,1)} %param.21) | copy-start | bytes 172036
  16.2 32.2 %all-to-all-start = ((bf16[32,8,224]{2,1,0:T(8,128)(2,1)}), bf16[32,8,224]{2,1,0:T(8,128)(2,1)S(1)}, u32[]{:S(2)}, u32[]{:S(2)}) async-start(bf16[32,8,224]{2,1,0:T(8,128)(2,1)} %select_bitcast_fusion.1), calls=%async_computation | async-start | bytes 262144 | tf_op jit(solution)/shard_map/all_to_all | solution.py:52
  48.4 19.4 %all-to-all-start.4 = ((bf16[32,8,224]{2,1,0:T(8,128)(2,1)}), bf16[32,8,224]{2,1,0:T(8,128)(2,1)S(1)}, u32[]{:S(2)}, u32[]{:S(2)}) async-start(bf16[32,8,224]{2,1,0:T(8,128)(2,1)} %fusion.21), calls=%async_computation.5 | async-start | bytes 262144 | tf_op jit(solution)/shard_map/all_to_all | solution.py:52
  53.3 22.9 %copy-start.7 = (s32[16]{0:T(128)S(1)}, s32[16]{0:T(128)}, u32[]{:S(2)}) copy-start(s32[16]{0:T(128)} %param.17) | copy-start | bytes 196
  69.3 8.6 %copy-start.2 = (bf16[16,112,128]{2,1,0:T(8,128)(2,1)S(1)}, bf16[16,112,128]{2,1,0:T(8,128)(2,1)}, u32[]{:S(2)}) copy-start(bf16[16,112,128]{2,1,0:T(8,128)(2,1)} %param.18) | copy-start | bytes 1376260
  69.3 33.3 %all-to-all-start.1 = ((bf16[16,256,224]{1,2,0:T(8,128)(2,1)}), bf16[16,256,224]{1,2,0:T(8,128)(2,1)S(1)}, u32[]{:S(2)}, u32[]{:S(2)}) async-start(bf16[16,256,224]{1,2,0:T(8,128)(2,1)} %stack.6), calls=%async_computation.1 | async-start | bytes 3670016 | tf_op jit(solution)/shard_map/all_to_all | solution.py:56
  102.5 1.2 copy-start.1
  103.8 132.4 %all-to-all-start.2 = ((bf16[32,112,384]{2,1,0:T(8,128)(2,1)}), bf16[32,112,384]{2,1,0:T(8,128)(2,1)S(1)}, u32[]{:S(2)}, u32[]{:S(2)}) async-start(bf16[32,112,384]{2,1,0:T(8,128)(2,1)} %pad_maximum_fusion), calls=%async_computation.2 | async-start | bytes 5505024 | tf_op jit(solution)/shard_map/all_to_all | solution.py:36
  237.6 32.4 %all-to-all-start.5 = ((bf16[16,256,224]{1,2,0:T(8,128)(2,1)}), bf16[16,256,224]{1,2,0:T(8,128)(2,1)}, u32[]{:S(2)}, u32[]{:S(2)}) async-start(bf16[16,256,224]{1,2,0:T(8,128)(2,1)} %stack.7), calls=%async_computation.6 | async-start | bytes 3670016 | tf_op jit(solution)/shard_map/all_to_all | solution.py:56
  243.6 113.6 %reduce-scatter.5.cloned.1.call-start = ((), (), s32[]{:S(2)}) async-start(), calls=%async_computation.11 | async-start | bytes 1949696 | tf_op jit(solution)/shard_map/reduce_scatter | solution.py:63
  274.1 180.8 %reduce-scatter.3.cloned.1.call-start = ((), (), s32[]{:S(2)}) async-start(), calls=%async_computation.10 | async-start | bytes 1949696 | tf_op jit(solution)/shard_map/reduce_scatter | solution.py:63
  358.8 97.7 %all-to-all-start.6 = ((bf16[32,8,224]{2,1,0:T(8,128)(2,1)}), bf16[32,8,224]{2,1,0:T(8,128)(2,1)S(1)}, u32[]{:S(2)}, u32[]{:S(2)}) async-start(bf16[32,8,224]{2,1,0:T(8,128)(2,1)} %bitcast.18), calls=%async_computation.8 | async-start | bytes 262144 | tf_op jit(solution)/shard_map/all_to_all | solution.py:69
  456.6 27.6 %all-to-all-start.3 = ((bf16[32,8,224]{2,1,0:T(8,128)(2,1)}), bf16[32,8,224]{2,1,0:T(8,128)(2,1)S(1)}, u32[]{:S(2)}, u32[]{:S(2)}) async-start(bf16[32,8,224]{2,1,0:T(8,128)(2,1)} %bitcast.11), calls=%async_computation.4 | async-start | bytes 262144 | tf_op jit(solution)/shard_map/all_to_all | solution.py:69
  474.7 15.1 %copy-start.5 = (s32[128,1]{0,1:T(1,128)S(1)}, s32[128,1]{0,1:T(1,128)}, u32[]{:S(2)}) copy-start(s32[128,1]{0,1:T(1,128)} %param.15) | copy-start | bytes 1540
  474.7 19.1 %copy-start.6 = (f32[128,1]{0,1:T(1,128)S(1)}, f32[128,1]{0,1:T(1,128)}, u32[]{:S(2)}) copy-start(f32[128,1]{0,1:T(1,128)} %param.16) | copy-start | bytes 1540
  484.1 0.7 copy-start.3
  484.8 129.1 %all-to-all-start.7 = ((bf16[32,112,384]{2,1,0:T(8,128)(2,1)}), bf16[32,112,384]{2,1,0:T(8,128)(2,1)S(1)}, u32[]{:S(2)}, u32[]{:S(2)}) async-start(bf16[32,112,384]{2,1,0:T(8,128)(2,1)} %copy.43), calls=%async_computation.9 | async-start | bytes 5505024 | tf_op jit(solution)/shard_map/all_to_all | solution.py:107
Sparse Core Ops, SparseCore 0:
  274.2 82.9 reduce-scatter.4
  362.7 92.1 reduce-scatter.2
